TPU v7x, 32 devices: a whole 2x2x4 slice. The times are simulated.
32 devices in a mesh: groups: 2 (over y), src: 4 (over z), dst: 4 (over x, core).
Axes of the slice: x: 2, y: 2, z: 4, core: 2. Of those that a mesh axis runs over, the one named last changes fastest.
Arguments:
- blocks: bfloat16 [20480, 128, 128], P(('groups', 'src', 'dst')), parts along dimension 0, may hold values from -1 to 1
- block_rows: int32 [20480], P(('groups', 'src', 'dst')), parts along dimension 0, may hold values from 0 to 255, as said below
- block_cols: int32 [20480], P(('groups', 'src', 'dst')), parts along dimension 0, may hold values from 0 to 127, as said below
- row_counts: int32 [65536], P(('groups', 'src')), parts along dimension 0, may hold values from 16 to 5952
- col_counts: int32 [32768], P(('groups', 'dst')), parts along dimension 0, may hold values from 16 to 5952
- start_panel: float32 [32, 32768], P(None, ('groups', 'dst')), parts along dimension 1, may hold values from -30 to 30
Outputs:
- coherent_panel: float32 [32, 32768], P(None, ('groups', 'dst')), parts along dimension 1
There are 2 independent parts, one for each index of `groups`. A program takes and returns all parts, laid end to end along the dimension named above; each array names one. Nothing has to cross between parts.
Inputs may be any that keep to these rules, and one draw needn't show every extreme that they name: `block_rows`: with q = j // 640, s = q // n and d = q % n (n devices along dst), entry j lies in block rows 64 * s to 64 * s + 63; every block row is named by exactly 40 entries, no two of them with the same block column. `block_cols`: with s and d as for block_rows, entry j lies in block columns 32 * d to 32 * d + 31; every block column is named by some entry.
All inputs are finite; a program needn't handle non-finite values.
Results may differ from a plain program's by a relative error of at most 0.0047.
Values may be sent and summed in bfloat16 or wider, within the bound.
A program may use at most 128 MiB of HBM per device.

v0:
```python
import functools

import jax
import jax.numpy as jnp
from jax import lax
from jax.experimental import pallas as pl
from jax.experimental.pallas import tpu as pltpu
from jax.sharding import PartitionSpec as P

ITERS = 2
UNROLL = 8
VMEM = pl.BlockSpec(memory_space=pltpu.VMEM)
SMEM = pl.BlockSpec(memory_space=pltpu.SMEM)
LIMIT = 48 * 1024 * 1024


def lanes(index, side):
    return pl.ds(pl.multiple_of(index * side, side), side)


def sweep_kernel(contract, gather_ref, scatter_ref, panel_ref, scale_ref, blocks_ref, out_ref, scaled):
    side = blocks_ref.shape[1]
    count = blocks_ref.shape[0]
    step = pl.program_id(0)

    @pl.when(step == 0)
    def _():
        scaled[...] = (panel_ref[...] / scale_ref[...]).astype(jnp.bfloat16)
        out_ref[...] = jnp.zeros_like(out_ref)

    @pl.loop(0, count // UNROLL)
    def _(chunk):
        terms = []
        for k in range(UNROLL):
            b = chunk * UNROLL + k
            g = gather_ref[step * count + b]
            terms.append(
                lax.dot_general(
                    scaled[:, lanes(g, side)],
                    blocks_ref[b],
                    (((1,), (contract,)), ((), ())),
                    preferred_element_type=jnp.float32,
                )
            )
        for k in range(UNROLL):
            s = scatter_ref[step * count + chunk * UNROLL + k]
            out_ref[:, lanes(s, side)] += terms[k]


def sweep(contract, gather_ids, scatter_ids, panel, scale, blocks, out_width):
    total, side, _ = blocks.shape
    count = 32 if total % 32 == 0 else UNROLL
    width = panel.shape[0]
    return pl.pallas_call(
        functools.partial(sweep_kernel, contract),
        grid=(total // count,),
        in_specs=[
            SMEM,
            SMEM,
            pl.BlockSpec(panel.shape, lambda i: (0, 0)),
            pl.BlockSpec(scale.shape, lambda i: (0, 0)),
            pl.BlockSpec((count, side, side), lambda i: (i, 0, 0)),
        ],
        out_specs=pl.BlockSpec((width, out_width), lambda i: (0, 0)),
        out_shape=jax.ShapeDtypeStruct((width, out_width), jnp.float32),
        scratch_shapes=[pltpu.VMEM(panel.shape, jnp.bfloat16)],
        compiler_params=pltpu.CompilerParams(vmem_limit_bytes=LIMIT),
    )(gather_ids, scatter_ids, panel, scale, blocks)


def gram(panel):
    return lax.dot_general(
        panel,
        panel,
        (((1,), (1,)), ((), ())),
        precision=lax.Precision.HIGHEST,
        preferred_element_type=jnp.float32,
    )


def inverse_factor(matrix):
    n = matrix.shape[0]
    row = lax.broadcasted_iota(jnp.int32, (n, n), 0)
    col = lax.broadcasted_iota(jnp.int32, (n, n), 1)
    both = jnp.concatenate([matrix, (row == col).astype(jnp.float32)], axis=1)
    row = lax.broadcasted_iota(jnp.int32, (n, 1), 0)
    for j in range(n):
        root = jnp.sqrt(both[j : j + 1, j : j + 1])
        pivot = both[j : j + 1, :] / root
        factor = both[:, j : j + 1] / root
        both = jnp.where(row == j, pivot, both - jnp.where(row > j, factor, 0.0) * pivot)
    return both[:, n:]


def apply(inverse, panel):
    return jnp.dot(
        inverse, panel, precision=lax.Precision.HIGHEST, preferred_element_type=jnp.float32
    )


def scale_gram_kernel(sums_ref, scale_ref, out_ref, gram_ref):
    out_ref[...] = sums_ref[...] / scale_ref[...]
    gram_ref[...] = gram(out_ref[...])


def apply_gram_kernel(box_total, gram_in_ref, panel_ref, out_ref, gram_ref):
    out_ref[...] = apply(inverse_factor(gram_in_ref[...] / box_total), panel_ref[...])
    gram_ref[...] = gram(out_ref[...])


def apply_kernel(box_total, gram_in_ref, panel_ref, out_ref):
    out_ref[...] = apply(inverse_factor(gram_in_ref[...] / box_total), panel_ref[...])


def small(kernel, outs, *args):
    return pl.pallas_call(
        kernel,
        in_specs=[VMEM] * len(args),
        out_specs=jax.tree.map(lambda _: VMEM, outs),
        out_shape=outs,
        compiler_params=pltpu.CompilerParams(vmem_limit_bytes=LIMIT),
    )(*args)


def per_device(blocks, block_rows, block_cols, row_counts, col_counts, start_panel):
    side = blocks.shape[1]
    width = start_panel.shape[0]
    rows = row_counts.shape[0]
    cols = col_counts.shape[0]
    box_total = float(cols * lax.axis_size("dst"))
    local_rows = block_rows - lax.axis_index("src") * (rows // side)
    local_cols = block_cols - lax.axis_index("dst") * (cols // side)
    row_scale = row_counts.astype(jnp.float32).reshape(1, rows)
    col_scale = jnp.sqrt(col_counts.astype(jnp.float32)).reshape(1, cols)
    panel = start_panel
    panel_type = jax.ShapeDtypeStruct((width, cols), jnp.float32)
    gram_type = jax.ShapeDtypeStruct((width, width), jnp.float32)
    for _ in range(ITERS):
        u = sweep(1, local_cols, local_rows, panel, col_scale, blocks, rows)
        u = lax.psum(u, "dst")
        w = sweep(0, local_rows, local_cols, u, row_scale, blocks, cols)
        w = lax.psum(w, "src")
        w, g = small(scale_gram_kernel, (panel_type, gram_type), w, col_scale)
        g = lax.psum(g, "dst")
        q, g = small(
            functools.partial(apply_gram_kernel, box_total), (panel_type, gram_type), g, w
        )
        g = lax.psum(g, "dst")
        panel = small(functools.partial(apply_kernel, box_total), panel_type, g, q)
    return panel


def solution(mesh):
    return jax.shard_map(
        per_device,
        mesh=mesh,
        in_specs=(
            P(("groups", "src", "dst"), None, None),
            P(("groups", "src", "dst")),
            P(("groups", "src", "dst")),
            P(("groups", "src")),
            P(("groups", "dst")),
            P(None, ("groups", "dst")),
        ),
        out_specs=P(None, ("groups", "dst")),
        check_vma=False,
    )
```

profile of v0, /device:TPU:0, one launch (start us, length us, event | category | flops | bytes accessed | tf_op | source)
XLA Modules:
  0.0 326.5 jit_solution(10107079169254063988)
XLA Ops:
  6.5 0.0 copy-start.5
  6.5 0.0 all-reduce.5.cloned.1.call-start
  6.5 0.7 convert_sqrt_fusion
  7.3 0.7 broadcast_subtract_fusion
  8.0 0.0 copy-start.2
  8.0 1.0 copy-done.2
  9.0 25.1 %shard_map.64 = f32[32,8192]{1,0:T(8,128)} custom-call(s32[640]{0:T(1024)S(1)} %get-tuple-element.21.gather_ref.scatter_ref, s32[640]{0:T(1024)S(1)} %get-tuple-element.22.scatter_ref.gather_ref, f32[32,4096]{1,0:T(8,128)S(1)} %copy-done.2, f32[1,4096]{1,0:T(1,128)S(1)} %bitcast.2, bf16[640,128,128]{2,1,0:T(8,128)(2,1)} %blocks_ref.7), custom_call_target="tpu_custom_call" | custom-call | tf_op jit(solution)/shard_map/pallas_call | solution.py:54
  34.1 0.0 all-reduce.5.cloned.1.call-update
  34.1 0.0 all-reduce.7.cloned.1.call-start
  34.2 0.0 copy-done.5
  34.2 38.8 %all-reduce.5.cloned.1.call-done.panel_ref = f32[32,8192]{1,0:T(8,128)} async-done(((f32[32,8192]{1,0:T(8,128)}), f32[32,8192]{1,0:T(8,128)}) %all-reduce.5.cloned.1.call-update) | async-done | bytes 1048592 | tf_op jit(solution)/shard_map/psum | solution.py:140
  73.0 0.0 copy-start.1
  73.0 1.2 copy-done.1
  74.3 22.4 %shard_map.65 = f32[32,4096]{1,0:T(8,128)} custom-call(s32[640]{0:T(1024)S(1)} %get-tuple-element.22.scatter_ref.gather_ref, s32[640]{0:T(1024)S(1)} %get-tuple-element.21.gather_ref.scatter_ref, f32[32,8192]{1,0:T(8,128)S(1)} %copy-done.1, f32[1,8192]{1,0:T(1,128)S(1)} %bitcast.6, bf16[640,128,128]{2,1,0:T(8,128)(2,1)} %blocks_ref.7), custom_call_target="tpu_custom_call" | custom-call | tf_op jit(solution)/shard_map/pallas_call | solution.py:54
  96.6 0.0 all-reduce.7.cloned.1.call-update
  96.6 0.0 all-reduce.9.cloned.1.call-start
  96.7 38.8 %all-reduce.7.cloned.1.call-done.sums_ref = f32[32,4096]{1,0:T(8,128)} async-done(((f32[32,4096]{1,0:T(8,128)}), f32[32,4096]{1,0:T(8,128)}) %all-reduce.7.cloned.1.call-update) | async-done | bytes 524304 | tf_op jit(solution)/shard_map/psum | solution.py:142
  135.5 0.0 copy-start.3
  135.5 1.0 copy-done.3
  136.5 0.6 shard_map.66
  137.1 10.2 %psum.58.gram_in_ref = f32[32,32]{1,0:T(8,128)S(1)} all-reduce(f32[32,32]{1,0:T(8,128)S(1)} %get-tuple-element.13), channel_id=1, replica_groups=mesh['groups'=2,'src'=4,'dst'=4] {'dst'}, use_global_device_ids=true, to_apply=%region_2.0 | all-reduce | flops 1024 | bytes 8192 | tf_op jit(solution)/shard_map/psum | solution.py:144
  147.3 4.3 %shard_map.67 = (f32[32,4096]{1,0:T(8,128)S(1)}, f32[32,32]{1,0:T(8,128)S(1)}) custom-call(f32[32,32]{1,0:T(8,128)S(1)} %psum.58.gram_in_ref, f32[32,4096]{1,0:T(8,128)S(1)} %get-tuple-element.14.panel_ref), custom_call_target="tpu_custom_call" | custom-call | tf_op jit(solution)/shard_map/pallas_call | solution.py:116
  151.6 10.1 %psum.59.gram_in_ref = f32[32,32]{1,0:T(8,128)S(1)} all-reduce(f32[32,32]{1,0:T(8,128)S(1)} %get-tuple-element.15), channel_id=1, replica_groups=mesh['groups'=2,'src'=4,'dst'=4] {'dst'}, use_global_device_ids=true, to_apply=%region_3.0 | all-reduce | flops 1024 | bytes 8192 | tf_op jit(solution)/shard_map/psum | solution.py:148
  161.7 3.7 %shard_map.68.panel_ref = f32[32,4096]{1,0:T(8,128)S(1)} custom-call(f32[32,32]{1,0:T(8,128)S(1)} %psum.59.gram_in_ref, f32[32,4096]{1,0:T(8,128)S(1)} %get-tuple-element.16.panel_ref), custom_call_target="tpu_custom_call" | custom-call | tf_op jit(solution)/shard_map/pallas_call | solution.py:116
  165.4 25.1 %shard_map.69 = f32[32,8192]{1,0:T(8,128)} custom-call(s32[640]{0:T(1024)S(1)} %get-tuple-element.21.gather_ref.scatter_ref, s32[640]{0:T(1024)S(1)} %get-tuple-element.22.scatter_ref.gather_ref, f32[32,4096]{1,0:T(8,128)S(1)} %shard_map.68.panel_ref, f32[1,4096]{1,0:T(1,128)S(1)} %bitcast.4, bf16[640,128,128]{2,1,0:T(8,128)(2,1)} %blocks_ref.7), custom_call_target="tpu_custom_call" | custom-call | tf_op jit(solution)/shard_map/pallas_call | solution.py:54
  190.5 0.0 all-reduce.9.cloned.1.call-update
  190.5 0.0 all-reduce.11.cloned.1.call-start
  190.5 36.3 %all-reduce.9.cloned.1.call-done.panel_ref = f32[32,8192]{1,0:T(8,128)} async-done(((f32[32,8192]{1,0:T(8,128)}), f32[32,8192]{1,0:T(8,128)}) %all-reduce.9.cloned.1.call-update) | async-done | bytes 1048592 | tf_op jit(solution)/shard_map/psum | solution.py:140
  226.8 0.0 copy-start
  226.8 1.2 copy-done
  228.0 22.4 %shard_map.70 = f32[32,4096]{1,0:T(8,128)} custom-call(s32[640]{0:T(1024)S(1)} %get-tuple-element.22.scatter_ref.gather_ref, s32[640]{0:T(1024)S(1)} %get-tuple-element.21.gather_ref.scatter_ref, f32[32,8192]{1,0:T(8,128)S(1)} %copy-done, f32[1,8192]{1,0:T(1,128)S(1)} %bitcast.7, bf16[640,128,128]{2,1,0:T(8,128)(2,1)} %blocks_ref.7), custom_call_target="tpu_custom_call" | custom-call | tf_op jit(solution)/shard_map/pallas_call | solution.py:54
  250.4 0.0 all-reduce.11.cloned.1.call-update
  250.4 38.8 %all-reduce.11.cloned.1.call-done.sums_ref = f32[32,4096]{1,0:T(8,128)} async-done(((f32[32,4096]{1,0:T(8,128)}), f32[32,4096]{1,0:T(8,128)}) %all-reduce.11.cloned.1.call-update) | async-done | bytes 524304 | tf_op jit(solution)/shard_map/psum | solution.py:142
  289.2 0.0 copy-start.4
  289.2 1.0 copy-done.4
  290.3 0.6 shard_map.71
  290.9 10.2 %psum.62.gram_in_ref = f32[32,32]{1,0:T(8,128)S(1)} all-reduce(f32[32,32]{1,0:T(8,128)S(1)} %get-tuple-element.17), channel_id=1, replica_groups=mesh['groups'=2,'src'=4,'dst'=4] {'dst'}, use_global_device_ids=true, to_apply=%region_6.0 | all-reduce | flops 1024 | bytes 8192 | tf_op jit(solution)/shard_map/psum | solution.py:144
  301.0 4.3 %shard_map.72 = (f32[32,4096]{1,0:T(8,128)S(1)}, f32[32,32]{1,0:T(8,128)S(1)}) custom-call(f32[32,32]{1,0:T(8,128)S(1)} %psum.62.gram_in_ref, f32[32,4096]{1,0:T(8,128)S(1)} %get-tuple-element.18.panel_ref), custom_call_target="tpu_custom_call" | custom-call | tf_op jit(solution)/shard_map/pallas_call | solution.py:116
  305.3 10.1 %psum.63.gram_in_ref = f32[32,32]{1,0:T(8,128)S(1)} all-reduce(f32[32,32]{1,0:T(8,128)S(1)} %get-tuple-element.19), channel_id=1, replica_groups=mesh['groups'=2,'src'=4,'dst'=4] {'dst'}, use_global_device_ids=true, to_apply=%region_7.0 | all-reduce | flops 1024 | bytes 8192 | tf_op jit(solution)/shard_map/psum | solution.py:148
  315.4 4.5 %shard_map.73 = f32[32,4096]{1,0:T(8,128)} custom-call(f32[32,32]{1,0:T(8,128)S(1)} %psum.63.gram_in_ref, f32[32,4096]{1,0:T(8,128)S(1)} %get-tuple-element.20.panel_ref), custom_call_target="tpu_custom_call" | custom-call | tf_op jit(solution)/shard_map/pallas_call | solution.py:116
  (1 shorter events, 0.0 us)
Async XLA Ops:
  6.5 27.6 %copy-start.5 = (s32[8192]{0:T(1024)S(1)}, s32[8192]{0:T(1024)}, u32[]{:S(2)}) copy-start(s32[8192]{0:T(1024)} %param.9) | copy-start | bytes 98308
  6.5 66.5 %all-reduce.5.cloned.1.call-start = ((), (), s32[]{:S(2)}) async-start(), calls=%async_computation | async-start | bytes 2097152 | tf_op jit(solution)/shard_map/psum | solution.py:140
  8.0 1.0 copy-start.2
  34.1 101.4 %all-reduce.7.cloned.1.call-start = ((), (), s32[]{:S(2)}) async-start(), calls=%async_computation.1 | async-start | bytes 1048576 | tf_op jit(solution)/shard_map/psum | solution.py:142
  73.0 1.2 copy-start.1
  96.6 130.2 %all-reduce.9.cloned.1.call-start = ((), (), s32[]{:S(2)}) async-start(), calls=%async_computation.2 | async-start | bytes 2097152 | tf_op jit(solution)/shard_map/psum | solution.py:140
  135.5 1.0 copy-start.3
  190.5 98.7 %all-reduce.11.cloned.1.call-start = ((), (), s32[]{:S(2)}) async-start(), calls=%async_computation.3 | async-start | bytes 1048576 | tf_op jit(solution)/shard_map/psum | solution.py:142
  226.8 1.2 copy-start
  289.2 1.0 copy-start.4
Sparse Core Ops, SparseCore 0:
  34.2 38.7 all-reduce.4
  96.8 38.6 all-reduce.6
  190.6 36.1 all-reduce.8
  250.5 38.6 all-reduce.10
where the time goes:
time: 329 us; the launch traced here: 326 us
  waiting for transfers between devices  153 us (47%)
  Pallas kernels  113 us (34%)
  blocking collectives  40.6 us (12%)
  between operations  13.2 us (4%)
  local copies, waits for them, and re-layouts  5.58 us (2%)
    pallas_call x4, Pallas kernels, sweep(): pl.pallas_call(functools.partial(sweep_kernel, contract), grid=(total //...  94.9 us
    psum x2, waiting for transfers between devices, per_device(): w = lax.psum(w, 'src')  77.6 us
    psum x2, waiting for transfers between devices, per_device(): u = lax.psum(u, 'dst')  75.1 us
    psum x4, blocking collectives, per_device(): g = lax.psum(g, 'dst')  40.6 us
    pallas_call x6, Pallas kernels, small(): pl.pallas_call(kernel, in_specs=[VMEM] * len(args), out_specs=jax.tree.ma...  17.9 us
  transfers between devices with their start and end apart: 4, of which 4 were waited for; matrix products, arithmetic and copies ran while one was open for 0% of the time, Pallas kernels for 0%

commit v1 on v0

--- a/solution.py
+++ b/solution.py
@@ -9,6 +9,7 @@
 
 ITERS = 2
 UNROLL = 8
+MESH = pl.DeviceIdType.MESH
 VMEM = pl.BlockSpec(memory_space=pltpu.VMEM)
 SMEM = pl.BlockSpec(memory_space=pltpu.SMEM)
 LIMIT = 48 * 1024 * 1024
@@ -18,14 +19,19 @@
     return pl.ds(pl.multiple_of(index * side, side), side)
 
 
-def sweep_kernel(contract, gather_ref, scatter_ref, panel_ref, scale_ref, blocks_ref, out_ref, scaled):
+def sweep_kernel(contract, gather_ref, scatter_ref, *refs):
+    if len(refs) == 5:
+        panel_ref, scale_ref, blocks_ref, out_ref, scaled = refs
+    else:
+        scaled, blocks_ref, out_ref = refs
     side = blocks_ref.shape[1]
     count = blocks_ref.shape[0]
     step = pl.program_id(0)
 
     @pl.when(step == 0)
     def _():
-        scaled[...] = (panel_ref[...] / scale_ref[...]).astype(jnp.bfloat16)
+        if len(refs) == 5:
+            scaled[...] = (panel_ref[...] / scale_ref[...]).astype(jnp.bfloat16)
         out_ref[...] = jnp.zeros_like(out_ref)
 
     @pl.loop(0, count // UNROLL)
@@ -51,21 +57,21 @@
     total, side, _ = blocks.shape
     count = 32 if total % 32 == 0 else UNROLL
     width = panel.shape[0]
+    small = [panel] if scale is None else [panel, scale]
     return pl.pallas_call(
         functools.partial(sweep_kernel, contract),
         grid=(total // count,),
         in_specs=[
             SMEM,
             SMEM,
-            pl.BlockSpec(panel.shape, lambda i: (0, 0)),
-            pl.BlockSpec(scale.shape, lambda i: (0, 0)),
+            *(pl.BlockSpec(a.shape, lambda i: (0, 0)) for a in small),
             pl.BlockSpec((count, side, side), lambda i: (i, 0, 0)),
         ],
         out_specs=pl.BlockSpec((width, out_width), lambda i: (0, 0)),
         out_shape=jax.ShapeDtypeStruct((width, out_width), jnp.float32),
-        scratch_shapes=[pltpu.VMEM(panel.shape, jnp.bfloat16)],
+        scratch_shapes=[pltpu.VMEM(panel.shape, jnp.bfloat16)] * (scale is not None),
         compiler_params=pltpu.CompilerParams(vmem_limit_bytes=LIMIT),
-    )(gather_ids, scatter_ids, panel, scale, blocks)
+    )(gather_ids, scatter_ids, *small, blocks)
 
 
 def gram(panel):
@@ -98,28 +104,186 @@
     )
 
 
-def scale_gram_kernel(sums_ref, scale_ref, out_ref, gram_ref):
-    out_ref[...] = sums_ref[...] / scale_ref[...]
-    gram_ref[...] = gram(out_ref[...])
-
-
-def apply_gram_kernel(box_total, gram_in_ref, panel_ref, out_ref, gram_ref):
-    out_ref[...] = apply(inverse_factor(gram_in_ref[...] / box_total), panel_ref[...])
-    gram_ref[...] = gram(out_ref[...])
-
-
-def apply_kernel(box_total, gram_in_ref, panel_ref, out_ref):
-    out_ref[...] = apply(inverse_factor(gram_in_ref[...] / box_total), panel_ref[...])
-
-
-def small(kernel, outs, *args):
+def greet(axes):
+    barrier = pltpu.get_barrier_semaphore()
+    number = 0
+    for axis in axes:
+        n = lax.axis_size(axis)
+        me = lax.axis_index(axis)
+        for k in range(1, n):
+            pl.semaphore_signal(
+                barrier, inc=1, device_id={axis: lax.rem(me + k, n)}, device_id_type=MESH
+            )
+            number += 1
+    pl.semaphore_wait(barrier, number)
+
+
+def scatter_sums(axis, sums_ref, half, landing, sems):
+    n = lax.axis_size(axis)
+    me = lax.axis_index(axis)
+    part = sums_ref.shape[1] // n
+    copies = []
+    for k in range(1, n):
+        peer = lax.rem(me + k, n)
+        copy = pltpu.make_async_remote_copy(
+            src_ref=half.at[:, lanes(peer, part)],
+            dst_ref=landing.at[k],
+            send_sem=sems.at[0, k],
+            recv_sem=sems.at[1, k],
+            device_id={axis: peer},
+            device_id_type=MESH,
+        )
+        copy.start()
+        copies.append(copy)
+    mine = lanes(me, part)
+    total = sums_ref[:, mine]
+    for k in range(1, n):
+        copies[k - 1].wait_recv()
+        total = total + landing[k].astype(jnp.float32)
+    return total, mine, copies
+
+
+def gather_start(axis, whole, mine, sems):
+    n = lax.axis_size(axis)
+    me = lax.axis_index(axis)
+    copies = []
+    for k in range(1, n):
+        copy = pltpu.make_async_remote_copy(
+            src_ref=whole.at[:, mine],
+            dst_ref=whole.at[:, mine],
+            send_sem=sems.at[0, k],
+            recv_sem=sems.at[1, k],
+            device_id={axis: lax.rem(me + k, n)},
+            device_id_type=MESH,
+        )
+        copy.start()
+        copies.append(copy)
+    return copies
+
+
+def sum_small(axis, value, slots, sems):
+    n = lax.axis_size(axis)
+    me = lax.axis_index(axis)
+    slots[me] = value
+    copies = []
+    for k in range(1, n):
+        copy = pltpu.make_async_remote_copy(
+            src_ref=slots.at[me],
+            dst_ref=slots.at[me],
+            send_sem=sems.at[0, k],
+            recv_sem=sems.at[1, k],
+            device_id={axis: lax.rem(me + k, n)},
+            device_id_type=MESH,
+        )
+        copy.start()
+        copies.append(copy)
+    for copy in copies:
+        copy.wait()
+    total = slots[0]
+    for k in range(1, n):
+        total = total + slots[k]
+    return total
+
+
+def rows_kernel(axis, sums_ref, scale_ref, out_ref, half, landing, whole, scatter_sems, gather_sems):
+    half[...] = sums_ref[...].astype(jnp.bfloat16)
+    greet((axis,))
+    total, mine, sent = scatter_sums(axis, sums_ref, half, landing, scatter_sems)
+    whole[:, mine] = (total / scale_ref[:, mine]).astype(jnp.bfloat16)
+    gathered = gather_start(axis, whole, mine, gather_sems)
+    for copy in sent:
+        copy.wait_send()
+    for copy in gathered:
+        copy.wait()
+    out_ref[...] = whole[...]
+
+
+def panel_kernel(
+    box_total,
+    sums_ref,
+    scale_ref,
+    out_ref,
+    half,
+    landing,
+    whole,
+    slots_src,
+    slots_dst,
+    slots_second,
+    scatter_sems,
+    gather_sems,
+    src_sems,
+    dst_sems,
+    second_sems,
+):
+    half[...] = sums_ref[...].astype(jnp.bfloat16)
+    greet(("src", "dst"))
+    total, mine, sent = scatter_sums("src", sums_ref, half, landing, scatter_sems)
+    own = total / scale_ref[:, mine]
+    whole[:, mine] = own
+    gathered = gather_start("src", whole, mine, gather_sems)
+    first = sum_small("src", gram(own), slots_src, src_sems)
+    first = sum_small("dst", first, slots_dst, dst_sems)
+    inverse = inverse_factor(first / box_total)
+    for copy in sent:
+        copy.wait_send()
+    for copy in gathered:
+        copy.wait()
+    out_ref[...] = apply(inverse, whole[...])
+    second = sum_small("dst", gram(out_ref[...]), slots_second, second_sems)
+    out_ref[...] = apply(inverse_factor(second / box_total), out_ref[...])
+
+
+def sem_pairs(n):
+    return pltpu.SemaphoreType.DMA((2, n))
+
+
+def reduce_rows(sums, scale):
+    n = lax.axis_size("dst")
+    width, extent = sums.shape
     return pl.pallas_call(
-        kernel,
-        in_specs=[VMEM] * len(args),
-        out_specs=jax.tree.map(lambda _: VMEM, outs),
-        out_shape=outs,
-        compiler_params=pltpu.CompilerParams(vmem_limit_bytes=LIMIT),
-    )(*args)
+        functools.partial(rows_kernel, "dst"),
+        in_specs=[VMEM] * 2,
+        out_specs=VMEM,
+        out_shape=jax.ShapeDtypeStruct(sums.shape, jnp.bfloat16),
+        scratch_shapes=[
+            pltpu.VMEM(sums.shape, jnp.bfloat16),
+            pltpu.VMEM((n, width, extent // n), jnp.bfloat16),
+            pltpu.VMEM(sums.shape, jnp.bfloat16),
+            sem_pairs(n),
+            sem_pairs(n),
+        ],
+        compiler_params=pltpu.CompilerParams(
+            collective_id=0, has_side_effects=True, vmem_limit_bytes=LIMIT
+        ),
+    )(sums, scale)
+
+
+def reduce_panel(sums, scale, box_total):
+    n_src = lax.axis_size("src")
+    n_dst = lax.axis_size("dst")
+    width, extent = sums.shape
+    return pl.pallas_call(
+        functools.partial(panel_kernel, box_total),
+        in_specs=[VMEM] * 2,
+        out_specs=VMEM,
+        out_shape=jax.ShapeDtypeStruct(sums.shape, jnp.float32),
+        scratch_shapes=[
+            pltpu.VMEM(sums.shape, jnp.bfloat16),
+            pltpu.VMEM((n_src, width, extent // n_src), jnp.bfloat16),
+            pltpu.VMEM(sums.shape, jnp.float32),
+            pltpu.VMEM((n_src, width, width), jnp.float32),
+            pltpu.VMEM((n_dst, width, width), jnp.float32),
+            pltpu.VMEM((n_dst, width, width), jnp.float32),
+            sem_pairs(n_src),
+            sem_pairs(n_src),
+            sem_pairs(n_src),
+            sem_pairs(n_dst),
+            sem_pairs(n_dst),
+        ],
+        compiler_params=pltpu.CompilerParams(
+            collective_id=1, has_side_effects=True, vmem_limit_bytes=LIMIT
+        ),
+    )(sums, scale)
 
 
 def per_device(blocks, block_rows, block_cols, row_counts, col_counts, start_panel):
@@ -133,20 +297,11 @@
     row_scale = row_counts.astype(jnp.float32).reshape(1, rows)
     col_scale = jnp.sqrt(col_counts.astype(jnp.float32)).reshape(1, cols)
     panel = start_panel
-    panel_type = jax.ShapeDtypeStruct((width, cols), jnp.float32)
-    gram_type = jax.ShapeDtypeStruct((width, width), jnp.float32)
     for _ in range(ITERS):
         u = sweep(1, local_cols, local_rows, panel, col_scale, blocks, rows)
-        u = lax.psum(u, "dst")
-        w = sweep(0, local_rows, local_cols, u, row_scale, blocks, cols)
-        w = lax.psum(w, "src")
-        w, g = small(scale_gram_kernel, (panel_type, gram_type), w, col_scale)
-        g = lax.psum(g, "dst")
-        q, g = small(
-            functools.partial(apply_gram_kernel, box_total), (panel_type, gram_type), g, w
-        )
-        g = lax.psum(g, "dst")
-        panel = small(functools.partial(apply_kernel, box_total), panel_type, g, q)
+        z = reduce_rows(u, row_scale)
+        w = sweep(0, local_rows, local_cols, z, None, blocks, cols)
+        panel = reduce_panel(w, col_scale, box_total)
     return panel
 
 

time: 329 us -> 204 us (0.62)
  waiting for transfers between devices: 153 us -> 0 us
  Pallas kernels: 113 us -> 197 us
  blocking collectives: 40.6 us -> 0 us
  between operations: 13.2 us -> 0.07 us
  local copies, waits for them, and re-layouts: 5.58 us -> 1.84 us
    psum x4 -> x0, waiting for transfers between devices: 153 us -> none  [the longest x2 77.6 us: per_device(): w = lax.psum(w, 'src')]
    pallas_call x6 -> x4, Pallas kernels: 17.9 us -> 106 us  [the longest x2 77.7 us: reduce_panel(): pl.pallas_call(functools.partial(panel_kernel, box_total), in_specs=[VMEM...]
    psum x4 -> x0, blocking collectives: 40.6 us -> none  [per_device(): g = lax.psum(g, 'dst')]
    pallas_call x4, Pallas kernels: 94.9 us -> 91.1 us  [sweep(): pl.pallas_call(functools.partial(sweep_kernel, contract), grid=(total //...]
    unnamed x12 -> x3, local copies, waits for them, and re-layouts: 5.58 us -> 1.84 us
  transfers between devices with their start and end apart: 4 -> 0, of which waited for: 4 -> 0; matrix products, arithmetic and copies ran while one was open for 0% -> 0% of each run, Pallas kernels for 0% -> 0%
where the time goes in v1:
time: 204 us; the launch traced here: 202 us
  Pallas kernels  197 us (97%)
  other arithmetic  2.2 us (1%)
    pallas_call x4, Pallas kernels, sweep(): pl.pallas_call(functools.partial(sweep_kernel, contract), grid=(total //...  91.1 us
    pallas_call x2, Pallas kernels, reduce_panel(): pl.pallas_call(functools.partial(panel_kernel, box_total), in_specs=[VMEM...  77.7 us
    pallas_call x2, Pallas kernels, reduce_rows(): pl.pallas_call(functools.partial(rows_kernel, 'dst'), in_specs=[VMEM] * 2...  28.6 us

profile of v1, /device:TPU:0, one launch (start us, length us, event | category | flops | bytes accessed | tf_op | source)
XLA Modules:
  0.0 201.5 jit_solution(10598541386198065142)
XLA Ops:
  0.0 0.7 broadcast_subtract_fusion
  0.7 0.7 convert_sqrt_fusion
  1.4 0.8 convert_element_type.7
  2.2 0.0 copy-start
  2.2 1.0 copy-done
  3.2 24.0 %shard_map.64.sums_ref = f32[32,8192]{1,0:T(8,128)S(1)} custom-call(s32[640]{0:T(1024)S(1)} %get-tuple-element.5.gather_ref.scatter_ref, s32[640]{0:T(1024)S(1)} %get-tuple-element.6.scatter_ref.gather_ref, f32[32,4096]{1,0:T(8,128)S(1)} %copy-done, f32[1,4096]{1,0:T(1,128)S(1)} %bitcast.2, bf16[640,128,128]{2,1,0:T(8,128)(2,1)} %refs_1_.3), custom_call_target="tpu_custom_call" | custom-call | tf_op jit(solution)/shard_map/pallas_call | solution.py:61
  27.3 15.3 %shard_map.65.refs_0_ = bf16[32,8192]{1,0:T(8,128)(2,1)S(1)} custom-call(f32[32,8192]{1,0:T(8,128)S(1)} %shard_map.64.sums_ref, f32[1,8192]{1,0:T(1,128)S(1)} %bitcast.6), custom_call_target="tpu_custom_call" | custom-call | tf_op jit(solution)/shard_map/pallas_call | solution.py:243
  42.6 21.5 %shard_map.66.sums_ref = f32[32,4096]{1,0:T(8,128)S(1)} custom-call(s32[640]{0:T(1024)S(1)} %get-tuple-element.6.scatter_ref.gather_ref, s32[640]{0:T(1024)S(1)} %get-tuple-element.5.gather_ref.scatter_ref, bf16[32,8192]{1,0:T(8,128)(2,1)S(1)} %shard_map.65.refs_0_, bf16[640,128,128]{2,1,0:T(8,128)(2,1)} %refs_1_.3), custom_call_target="tpu_custom_call" | custom-call | tf_op jit(solution)/shard_map/pallas_call | solution.py:61
  64.1 39.0 %shard_map.67.refs_0_ = f32[32,4096]{1,0:T(8,128)S(1)} custom-call(f32[32,4096]{1,0:T(8,128)S(1)} %shard_map.66.sums_ref, f32[1,4096]{1,0:T(1,128)S(1)} %bitcast.3), custom_call_target="tpu_custom_call" | custom-call | tf_op jit(solution)/shard_map/pallas_call | solution.py:265
  103.1 24.1 %shard_map.68.sums_ref = f32[32,8192]{1,0:T(8,128)S(1)} custom-call(s32[640]{0:T(1024)S(1)} %get-tuple-element.5.gather_ref.scatter_ref, s32[640]{0:T(1024)S(1)} %get-tuple-element.6.scatter_ref.gather_ref, f32[32,4096]{1,0:T(8,128)S(1)} %shard_map.67.refs_0_, f32[1,4096]{1,0:T(1,128)S(1)} %bitcast.4, bf16[640,128,128]{2,1,0:T(8,128)(2,1)} %refs_1_.3), custom_call_target="tpu_custom_call" | custom-call | tf_op jit(solution)/shard_map/pallas_call | solution.py:61
  127.2 13.3 %shard_map.69.refs_0_ = bf16[32,8192]{1,0:T(8,128)(2,1)S(1)} custom-call(f32[32,8192]{1,0:T(8,128)S(1)} %shard_map.68.sums_ref, f32[1,8192]{1,0:T(1,128)S(1)} %bitcast.7), custom_call_target="tpu_custom_call" | custom-call | tf_op jit(solution)/shard_map/pallas_call | solution.py:243
  140.5 21.5 %shard_map.70.sums_ref = f32[32,4096]{1,0:T(8,128)S(1)} custom-call(s32[640]{0:T(1024)S(1)} %get-tuple-element.6.scatter_ref.gather_ref, s32[640]{0:T(1024)S(1)} %get-tuple-element.5.gather_ref.scatter_ref, bf16[32,8192]{1,0:T(8,128)(2,1)S(1)} %shard_map.69.refs_0_, bf16[640,128,128]{2,1,0:T(8,128)(2,1)} %refs_1_.3), custom_call_target="tpu_custom_call" | custom-call | tf_op jit(solution)/shard_map/pallas_call | solution.py:61
  162.0 38.7 %shard_map.71 = f32[32,4096]{1,0:T(8,128)S(1)} custom-call(f32[32,4096]{1,0:T(8,128)S(1)} %shard_map.70.sums_ref, f32[1,4096]{1,0:T(1,128)S(1)} %bitcast.5), custom_call_target="tpu_custom_call" | custom-call | tf_op jit(solution)/shard_map/pallas_call | solution.py:265
  200.7 0.8 copy.8
Async XLA Ops:
  2.2 1.0 copy-start

commit v2 on v1

--- a/solution.py
+++ b/solution.py
@@ -8,7 +8,7 @@
 from jax.sharding import PartitionSpec as P
 
 ITERS = 2
-UNROLL = 8
+CHUNKS = (128, 64, 32, 16, 8)
 MESH = pl.DeviceIdType.MESH
 VMEM = pl.BlockSpec(memory_space=pltpu.VMEM)
 SMEM = pl.BlockSpec(memory_space=pltpu.SMEM)
@@ -19,7 +19,11 @@
     return pl.ds(pl.multiple_of(index * side, side), side)
 
 
-def sweep_kernel(contract, gather_ref, scatter_ref, *refs):
+def root_of(counts):
+    return jnp.sqrt(counts.astype(jnp.float32))
+
+
+def sweep_kernel(contract, unroll, gather_ref, scatter_ref, *refs):
     if len(refs) == 5:
         panel_ref, scale_ref, blocks_ref, out_ref, scaled = refs
     else:
@@ -31,15 +35,15 @@
     @pl.when(step == 0)
     def _():
         if len(refs) == 5:
-            scaled[...] = (panel_ref[...] / scale_ref[...]).astype(jnp.bfloat16)
+            scaled[...] = (panel_ref[...] / root_of(scale_ref[...])).astype(jnp.bfloat16)
         out_ref[...] = jnp.zeros_like(out_ref)
 
-    @pl.loop(0, count // UNROLL)
+    @pl.loop(0, count // unroll)
     def _(chunk):
         terms = []
-        for k in range(UNROLL):
-            b = chunk * UNROLL + k
-            g = gather_ref[step * count + b]
+        for k in range(unroll):
+            b = chunk * unroll + k
+            g = lax.rem(gather_ref[step * count + b], scaled.shape[1] // side)
             terms.append(
                 lax.dot_general(
                     scaled[:, lanes(g, side)],
@@ -48,18 +52,19 @@
                     preferred_element_type=jnp.float32,
                 )
             )
-        for k in range(UNROLL):
-            s = scatter_ref[step * count + chunk * UNROLL + k]
+        for k in range(unroll):
+            s = lax.rem(scatter_ref[step * count + chunk * unroll + k], out_ref.shape[1] // side)
             out_ref[:, lanes(s, side)] += terms[k]
 
 
 def sweep(contract, gather_ids, scatter_ids, panel, scale, blocks, out_width):
     total, side, _ = blocks.shape
-    count = 32 if total % 32 == 0 else UNROLL
+    count = next(c for c in (*CHUNKS, 1) if total % c == 0)
+    unroll = min(count, 64)
     width = panel.shape[0]
     small = [panel] if scale is None else [panel, scale]
     return pl.pallas_call(
-        functools.partial(sweep_kernel, contract),
+        functools.partial(sweep_kernel, contract, unroll),
         grid=(total // count,),
         in_specs=[
             SMEM,
@@ -88,14 +93,15 @@
     n = matrix.shape[0]
     row = lax.broadcasted_iota(jnp.int32, (n, n), 0)
     col = lax.broadcasted_iota(jnp.int32, (n, n), 1)
-    both = jnp.concatenate([matrix, (row == col).astype(jnp.float32)], axis=1)
-    row = lax.broadcasted_iota(jnp.int32, (n, 1), 0)
-    for j in range(n):
-        root = jnp.sqrt(both[j : j + 1, j : j + 1])
-        pivot = both[j : j + 1, :] / root
-        factor = both[:, j : j + 1] / root
-        both = jnp.where(row == j, pivot, both - jnp.where(row > j, factor, 0.0) * pivot)
-    return both[:, n:]
+    diagonal = row == col
+    both = jnp.concatenate([matrix, diagonal.astype(jnp.float32)], axis=1)
+    row = lax.broadcasted_iota(jnp.int32, both.shape, 0)
+    for j in range(n - 1):
+        factor = jnp.broadcast_to(both[:, j : j + 1], both.shape)
+        pivot = both[j : j + 1, :] / factor[j : j + 1, :]
+        both = both - jnp.where(row > j, factor, 0.0) * pivot
+    pivots = jnp.sum(jnp.where(diagonal, both[:, :n], 0.0), axis=1, keepdims=True)
+    return both[:, n:] / jnp.sqrt(pivots)
 
 
 def apply(inverse, panel):
@@ -189,7 +195,7 @@
     half[...] = sums_ref[...].astype(jnp.bfloat16)
     greet((axis,))
     total, mine, sent = scatter_sums(axis, sums_ref, half, landing, scatter_sems)
-    whole[:, mine] = (total / scale_ref[:, mine]).astype(jnp.bfloat16)
+    whole[:, mine] = (total / scale_ref[:, mine].astype(jnp.float32)).astype(jnp.bfloat16)
     gathered = gather_start(axis, whole, mine, gather_sems)
     for copy in sent:
         copy.wait_send()
@@ -218,7 +224,7 @@
     half[...] = sums_ref[...].astype(jnp.bfloat16)
     greet(("src", "dst"))
     total, mine, sent = scatter_sums("src", sums_ref, half, landing, scatter_sems)
-    own = total / scale_ref[:, mine]
+    own = total / root_of(scale_ref[:, mine])
     whole[:, mine] = own
     gathered = gather_start("src", whole, mine, gather_sems)
     first = sum_small("src", gram(own), slots_src, src_sems)
@@ -287,20 +293,16 @@
 
 
 def per_device(blocks, block_rows, block_cols, row_counts, col_counts, start_panel):
-    side = blocks.shape[1]
-    width = start_panel.shape[0]
     rows = row_counts.shape[0]
     cols = col_counts.shape[0]
     box_total = float(cols * lax.axis_size("dst"))
-    local_rows = block_rows - lax.axis_index("src") * (rows // side)
-    local_cols = block_cols - lax.axis_index("dst") * (cols // side)
-    row_scale = row_counts.astype(jnp.float32).reshape(1, rows)
-    col_scale = jnp.sqrt(col_counts.astype(jnp.float32)).reshape(1, cols)
+    row_scale = row_counts.reshape(1, rows)
+    col_scale = col_counts.reshape(1, cols)
     panel = start_panel
     for _ in range(ITERS):
-        u = sweep(1, local_cols, local_rows, panel, col_scale, blocks, rows)
+        u = sweep(1, block_cols, block_rows, panel, col_scale, blocks, rows)
         z = reduce_rows(u, row_scale)
-        w = sweep(0, local_rows, local_cols, z, None, blocks, cols)
+        w = sweep(0, block_rows, block_cols, z, None, blocks, cols)
         panel = reduce_panel(w, col_scale, box_total)
     return panel
 

time: 204 us -> 161 us (0.79)
  Pallas kernels: 197 us -> 156 us
  other arithmetic: 2.2 us -> 0 us
  local copies, waits for them, and re-layouts: 1.84 us -> 3.93 us
    pallas_call x4, Pallas kernels: 91.1 us -> 51.3 us  [sweep(): pl.pallas_call(functools.partial(sweep_kernel, contract, unroll), grid=(t...]
    unnamed x3 -> x13, local copies, waits for them, and re-layouts: 1.84 us -> 3.93 us
where the time goes in v2:
time: 161 us; the launch traced here: 160 us
  Pallas kernels  156 us (97%)
  local copies, waits for them, and re-layouts  3.93 us (2%)
    pallas_call x2, Pallas kernels, reduce_panel(): pl.pallas_call(functools.partial(panel_kernel, box_total), in_specs=[VMEM...  76.2 us
    pallas_call x4, Pallas kernels, sweep(): pl.pallas_call(functools.partial(sweep_kernel, contract, unroll), grid=(t...  51.3 us
    pallas_call x2, Pallas kernels, reduce_rows(): pl.pallas_call(functools.partial(rows_kernel, 'dst'), in_specs=[VMEM] * 2...  28.7 us
    unnamed x13, local copies, waits for them, and re-layouts  3.93 us

profile of v2, /device:TPU:0, one launch (start us, length us, event | category | flops | bytes accessed | tf_op | source)
XLA Modules:
  0.0 160.2 jit_solution(7337562471037549782)
XLA Ops:
  0.0 0.0 copy-start
  0.0 1.0 copy-done
  1.0 0.0 copy-start.1
  1.0 0.7 copy-done.1
  1.8 0.0 copy-start.4
  1.8 0.7 copy-done.4
  2.4 0.0 copy-start.5
  2.5 0.7 copy-done.5
  3.1 0.0 copy-start.3
  3.1 0.0 copy-start.2
  3.1 14.7 %shard_map.64.sums_ref = f32[32,8192]{1,0:T(8,128)S(1)} custom-call(s32[640]{0:T(1024)S(1)} %copy-done.5, s32[640]{0:T(1024)S(1)} %copy-done.4, f32[32,4096]{1,0:T(8,128)S(1)} %copy-done, s32[1,4096]{1,0:T(1,128)S(1)} %bitcast.2, bf16[640,128,128]{2,1,0:T(8,128)(2,1)} %refs_1_.3), custom_call_target="tpu_custom_call" | custom-call | tf_op jit(solution)/shard_map/pallas_call | solution.py:66
  17.8 0.0 copy-done.3
  17.8 15.3 %shard_map.65.refs_0_ = bf16[32,8192]{1,0:T(8,128)(2,1)S(1)} custom-call(f32[32,8192]{1,0:T(8,128)S(1)} %shard_map.64.sums_ref, s32[1,8192]{1,0:T(1,128)S(1)} %bitcast.6), custom_call_target="tpu_custom_call" | custom-call | tf_op jit(solution)/shard_map/pallas_call | solution.py:249
  33.1 11.0 %shard_map.66.sums_ref = f32[32,4096]{1,0:T(8,128)S(1)} custom-call(s32[640]{0:T(1024)S(1)} %copy-done.4, s32[640]{0:T(1024)S(1)} %copy-done.5, bf16[32,8192]{1,0:T(8,128)(2,1)S(1)} %shard_map.65.refs_0_, bf16[640,128,128]{2,1,0:T(8,128)(2,1)} %refs_1_.3), custom_call_target="tpu_custom_call" | custom-call | tf_op jit(solution)/shard_map/pallas_call | solution.py:66
  44.2 0.0 copy-done.2
  44.2 38.2 %shard_map.67.refs_0_ = f32[32,4096]{1,0:T(8,128)S(1)} custom-call(f32[32,4096]{1,0:T(8,128)S(1)} %shard_map.66.sums_ref, s32[1,4096]{1,0:T(1,128)S(1)} %bitcast.3), custom_call_target="tpu_custom_call" | custom-call | tf_op jit(solution)/shard_map/pallas_call | solution.py:271
  82.4 14.7 %shard_map.68.sums_ref = f32[32,8192]{1,0:T(8,128)S(1)} custom-call(s32[640]{0:T(1024)S(1)} %copy-done.5, s32[640]{0:T(1024)S(1)} %copy-done.4, f32[32,4096]{1,0:T(8,128)S(1)} %shard_map.67.refs_0_, s32[1,4096]{1,0:T(1,128)S(1)} %bitcast.4, bf16[640,128,128]{2,1,0:T(8,128)(2,1)} %refs_1_.3), custom_call_target="tpu_custom_call" | custom-call | tf_op jit(solution)/shard_map/pallas_call | solution.py:66
  97.1 13.3 %shard_map.69.refs_0_ = bf16[32,8192]{1,0:T(8,128)(2,1)S(1)} custom-call(f32[32,8192]{1,0:T(8,128)S(1)} %shard_map.68.sums_ref, s32[1,8192]{1,0:T(1,128)S(1)} %bitcast.7), custom_call_target="tpu_custom_call" | custom-call | tf_op jit(solution)/shard_map/pallas_call | solution.py:249
  110.4 11.0 %shard_map.70.sums_ref = f32[32,4096]{1,0:T(8,128)S(1)} custom-call(s32[640]{0:T(1024)S(1)} %copy-done.4, s32[640]{0:T(1024)S(1)} %copy-done.5, bf16[32,8192]{1,0:T(8,128)(2,1)S(1)} %shard_map.69.refs_0_, bf16[640,128,128]{2,1,0:T(8,128)(2,1)} %refs_1_.3), custom_call_target="tpu_custom_call" | custom-call | tf_op jit(solution)/shard_map/pallas_call | solution.py:66
  121.4 37.9 %shard_map.71 = f32[32,4096]{1,0:T(8,128)S(1)} custom-call(f32[32,4096]{1,0:T(8,128)S(1)} %shard_map.70.sums_ref, s32[1,4096]{1,0:T(1,128)S(1)} %bitcast.5), custom_call_target="tpu_custom_call" | custom-call | tf_op jit(solution)/shard_map/pallas_call | solution.py:271
  159.4 0.8 copy.8
Async XLA Ops:
  0.0 1.0 copy-start
  1.0 0.7 copy-start.1
  1.8 0.7 copy-start.4
  2.4 0.7 copy-start.5
  3.1 14.7 %copy-start.3 = (s32[8192]{0:T(1024)S(1)}, s32[8192]{0:T(1024)}, u32[]{:S(2)}) copy-start(s32[8192]{0:T(1024)} %param.9) | copy-start | bytes 98308
  3.1 41.0 %copy-start.2 = (s32[4096]{0:T(1024)S(1)}, s32[4096]{0:T(1024)}, u32[]{:S(2)}) copy-start(s32[4096]{0:T(1024)} %param.10) | copy-start | bytes 49156

commit v3 on v2

--- a/solution.py
+++ b/solution.py
@@ -8,11 +8,11 @@
 from jax.sharding import PartitionSpec as P
 
 ITERS = 2
-CHUNKS = (128, 64, 32, 16, 8)
+CHUNKS = (64, 32, 16, 8)
 MESH = pl.DeviceIdType.MESH
 VMEM = pl.BlockSpec(memory_space=pltpu.VMEM)
 SMEM = pl.BlockSpec(memory_space=pltpu.SMEM)
-LIMIT = 48 * 1024 * 1024
+LIMIT = 24 * 1024 * 1024
 
 
 def lanes(index, side):
@@ -23,27 +23,31 @@
     return jnp.sqrt(counts.astype(jnp.float32))
 
 
-def sweep_kernel(contract, unroll, gather_ref, scatter_ref, *refs):
-    if len(refs) == 5:
-        panel_ref, scale_ref, blocks_ref, out_ref, scaled = refs
+def sweep_kernel(contract, unroll, gather_ref, scatter_ref, panel_ref, *refs):
+    if len(refs) == 6:
+        scale_ref, source_ref, out_ref, blocks_ref, sems, scaled = refs
     else:
-        scaled, blocks_ref, out_ref = refs
-    side = blocks_ref.shape[1]
-    count = blocks_ref.shape[0]
-    step = pl.program_id(0)
-
-    @pl.when(step == 0)
-    def _():
-        if len(refs) == 5:
-            scaled[...] = (panel_ref[...] / root_of(scale_ref[...])).astype(jnp.bfloat16)
-        out_ref[...] = jnp.zeros_like(out_ref)
-
-    @pl.loop(0, count // unroll)
+        source_ref, out_ref, blocks_ref, sems = refs
+        scaled = panel_ref
+    total, side, _ = blocks_ref.shape
+
+    def fetch(chunk):
+        place = pl.ds(chunk * unroll, unroll)
+        return pltpu.make_async_copy(source_ref.at[place], blocks_ref.at[place], sems.at[chunk])
+
+    for chunk in range(total // unroll):
+        fetch(chunk).start()
+    if len(refs) == 6:
+        scaled[...] = (panel_ref[...] / root_of(scale_ref[...])).astype(jnp.bfloat16)
+    out_ref[...] = jnp.zeros_like(out_ref)
+
+    @pl.loop(0, total // unroll)
     def _(chunk):
+        fetch(chunk).wait()
         terms = []
         for k in range(unroll):
             b = chunk * unroll + k
-            g = lax.rem(gather_ref[step * count + b], scaled.shape[1] // side)
+            g = lax.rem(gather_ref[b], scaled.shape[1] // side)
             terms.append(
                 lax.dot_general(
                     scaled[:, lanes(g, side)],
@@ -53,29 +57,24 @@
                 )
             )
         for k in range(unroll):
-            s = lax.rem(scatter_ref[step * count + chunk * unroll + k], out_ref.shape[1] // side)
+            s = lax.rem(scatter_ref[chunk * unroll + k], out_ref.shape[1] // side)
             out_ref[:, lanes(s, side)] += terms[k]
 
 
 def sweep(contract, gather_ids, scatter_ids, panel, scale, blocks, out_width):
-    total, side, _ = blocks.shape
-    count = next(c for c in (*CHUNKS, 1) if total % c == 0)
-    unroll = min(count, 64)
-    width = panel.shape[0]
+    unroll = next(c for c in (*CHUNKS, 1) if blocks.shape[0] % c == 0)
     small = [panel] if scale is None else [panel, scale]
     return pl.pallas_call(
         functools.partial(sweep_kernel, contract, unroll),
-        grid=(total // count,),
-        in_specs=[
-            SMEM,
-            SMEM,
-            *(pl.BlockSpec(a.shape, lambda i: (0, 0)) for a in small),
-            pl.BlockSpec((count, side, side), lambda i: (i, 0, 0)),
+        in_specs=[SMEM, SMEM, *(VMEM for _ in small), pl.BlockSpec(memory_space=pltpu.HBM)],
+        out_specs=VMEM,
+        out_shape=jax.ShapeDtypeStruct((panel.shape[0], out_width), jnp.float32),
+        scratch_shapes=[
+            pltpu.VMEM(blocks.shape, blocks.dtype),
+            pltpu.SemaphoreType.DMA((blocks.shape[0] // unroll,)),
+            *(pltpu.VMEM(panel.shape, jnp.bfloat16) for _ in small[1:]),
         ],
-        out_specs=pl.BlockSpec((width, out_width), lambda i: (0, 0)),
-        out_shape=jax.ShapeDtypeStruct((width, out_width), jnp.float32),
-        scratch_shapes=[pltpu.VMEM(panel.shape, jnp.bfloat16)] * (scale is not None),
-        compiler_params=pltpu.CompilerParams(vmem_limit_bytes=LIMIT),
+        compiler_params=pltpu.CompilerParams(vmem_limit_bytes=2 * LIMIT),
     )(gather_ids, scatter_ids, *small, blocks)
 
 
@@ -224,17 +223,17 @@
     half[...] = sums_ref[...].astype(jnp.bfloat16)
     greet(("src", "dst"))
     total, mine, sent = scatter_sums("src", sums_ref, half, landing, scatter_sems)
-    own = total / root_of(scale_ref[:, mine])
+    own = (total / root_of(scale_ref[:, mine])).astype(jnp.bfloat16)
     whole[:, mine] = own
     gathered = gather_start("src", whole, mine, gather_sems)
-    first = sum_small("src", gram(own), slots_src, src_sems)
+    first = sum_small("src", gram(own.astype(jnp.float32)), slots_src, src_sems)
     first = sum_small("dst", first, slots_dst, dst_sems)
     inverse = inverse_factor(first / box_total)
     for copy in sent:
         copy.wait_send()
     for copy in gathered:
         copy.wait()
-    out_ref[...] = apply(inverse, whole[...])
+    out_ref[...] = apply(inverse, whole[...].astype(jnp.float32))
     second = sum_small("dst", gram(out_ref[...]), slots_second, second_sems)
     out_ref[...] = apply(inverse_factor(second / box_total), out_ref[...])
 
@@ -276,7 +275,7 @@
         scratch_shapes=[
             pltpu.VMEM(sums.shape, jnp.bfloat16),
             pltpu.VMEM((n_src, width, extent // n_src), jnp.bfloat16),
-            pltpu.VMEM(sums.shape, jnp.float32),
+            pltpu.VMEM(sums.shape, jnp.bfloat16),
             pltpu.VMEM((n_src, width, width), jnp.float32),
             pltpu.VMEM((n_dst, width, width), jnp.float32),
             pltpu.VMEM((n_dst, width, width), jnp.float32),

time: 161 us -> 146 us (0.907)
  Pallas kernels: 156 us -> 142 us
    pallas_call x2, Pallas kernels: 76.2 us -> 65.8 us  [reduce_panel(): pl.pallas_call(functools.partial(panel_kernel, box_total), in_specs=[VMEM...]
    pallas_call x4, Pallas kernels: 51.3 us -> 47.5 us  [sweep(): pl.pallas_call(functools.partial(sweep_kernel, contract, unroll), in_spec...]
where the time goes in v3:
time: 146 us
  Pallas kernels  142 us (97%)
  local copies, waits for them, and re-layouts  3.93 us (3%)
    pallas_call x2, Pallas kernels, reduce_panel(): pl.pallas_call(functools.partial(panel_kernel, box_total), in_specs=[VMEM...  65.8 us
    pallas_call x4, Pallas kernels, sweep(): pl.pallas_call(functools.partial(sweep_kernel, contract, unroll), in_spec...  47.5 us
    pallas_call x2, Pallas kernels, reduce_rows(): pl.pallas_call(functools.partial(rows_kernel, 'dst'), in_specs=[VMEM] * 2...  28.3 us
    unnamed x13, local copies, waits for them, and re-layouts  3.93 us

profile of v3, /device:TPU:0, one launch (start us, length us, event | category | flops | bytes accessed | tf_op | source)
XLA Modules:
  0.0 145.6 jit_solution(16558069245213072486)
XLA Ops:
  0.0 0.0 copy-start
  0.0 1.0 copy-done
  1.0 0.0 copy-start.1
  1.0 0.7 copy-done.1
  1.8 0.0 copy-start.4
  1.8 0.7 copy-done.4
  2.4 0.0 copy-start.5
  2.5 0.7 copy-done.5
  3.1 0.0 copy-start.3
  3.1 0.0 copy-start.2
  3.1 14.5 %shard_map.64.sums_ref = f32[32,8192]{1,0:T(8,128)S(1)} custom-call(s32[640]{0:T(1024)S(1)} %copy-done.5, s32[640]{0:T(1024)S(1)} %copy-done.4, f32[32,4096]{1,0:T(8,128)S(1)} %copy-done, s32[1,4096]{1,0:T(1,128)S(1)} %bitcast.2, bf16[640,128,128]{2,1,0:T(8,128)(2,1)} %refs_0_.3), custom_call_target="tpu_custom_call" | custom-call | tf_op jit(solution)/shard_map/pallas_call | solution.py:67
  17.7 0.0 copy-done.3
  17.7 15.3 %shard_map.65.panel_ref = bf16[32,8192]{1,0:T(8,128)(2,1)S(1)} custom-call(f32[32,8192]{1,0:T(8,128)S(1)} %shard_map.64.sums_ref, s32[1,8192]{1,0:T(1,128)S(1)} %bitcast.6), custom_call_target="tpu_custom_call" | custom-call | tf_op jit(solution)/shard_map/pallas_call | solution.py:248
  33.0 9.2 %shard_map.66.sums_ref = f32[32,4096]{1,0:T(8,128)S(1)} custom-call(s32[640]{0:T(1024)S(1)} %copy-done.4, s32[640]{0:T(1024)S(1)} %copy-done.5, bf16[32,8192]{1,0:T(8,128)(2,1)S(1)} %shard_map.65.panel_ref, bf16[640,128,128]{2,1,0:T(8,128)(2,1)} %refs_0_.3), custom_call_target="tpu_custom_call" | custom-call | tf_op jit(solution)/shard_map/pallas_call | solution.py:67
  42.2 0.0 copy-done.2
  42.2 33.2 %shard_map.67.panel_ref = f32[32,4096]{1,0:T(8,128)S(1)} custom-call(f32[32,4096]{1,0:T(8,128)S(1)} %shard_map.66.sums_ref, s32[1,4096]{1,0:T(1,128)S(1)} %bitcast.3), custom_call_target="tpu_custom_call" | custom-call | tf_op jit(solution)/shard_map/pallas_call | solution.py:270
  75.4 14.5 %shard_map.68.sums_ref = f32[32,8192]{1,0:T(8,128)S(1)} custom-call(s32[640]{0:T(1024)S(1)} %copy-done.5, s32[640]{0:T(1024)S(1)} %copy-done.4, f32[32,4096]{1,0:T(8,128)S(1)} %shard_map.67.panel_ref, s32[1,4096]{1,0:T(1,128)S(1)} %bitcast.4, bf16[640,128,128]{2,1,0:T(8,128)(2,1)} %refs_0_.3), custom_call_target="tpu_custom_call" | custom-call | tf_op jit(solution)/shard_map/pallas_call | solution.py:67
  90.0 13.0 %shard_map.69.panel_ref = bf16[32,8192]{1,0:T(8,128)(2,1)S(1)} custom-call(f32[32,8192]{1,0:T(8,128)S(1)} %shard_map.68.sums_ref, s32[1,8192]{1,0:T(1,128)S(1)} %bitcast.7), custom_call_target="tpu_custom_call" | custom-call | tf_op jit(solution)/shard_map/pallas_call | solution.py:248
  103.0 9.2 %shard_map.70.sums_ref = f32[32,4096]{1,0:T(8,128)S(1)} custom-call(s32[640]{0:T(1024)S(1)} %copy-done.4, s32[640]{0:T(1024)S(1)} %copy-done.5, bf16[32,8192]{1,0:T(8,128)(2,1)S(1)} %shard_map.69.panel_ref, bf16[640,128,128]{2,1,0:T(8,128)(2,1)} %refs_0_.3), custom_call_target="tpu_custom_call" | custom-call | tf_op jit(solution)/shard_map/pallas_call | solution.py:67
  112.2 32.6 %shard_map.71 = f32[32,4096]{1,0:T(8,128)S(1)} custom-call(f32[32,4096]{1,0:T(8,128)S(1)} %shard_map.70.sums_ref, s32[1,4096]{1,0:T(1,128)S(1)} %bitcast.5), custom_call_target="tpu_custom_call" | custom-call | tf_op jit(solution)/shard_map/pallas_call | solution.py:270
  144.8 0.8 copy.8
Async XLA Ops:
  0.0 1.0 copy-start
  1.0 0.7 copy-start.1
  1.8 0.7 copy-start.4
  2.4 0.7 copy-start.5
  3.1 14.5 %copy-start.3 = (s32[8192]{0:T(1024)S(1)}, s32[8192]{0:T(1024)}, u32[]{:S(2)}) copy-start(s32[8192]{0:T(1024)} %param.9) | copy-start | bytes 98308
  3.1 39.1 %copy-start.2 = (s32[4096]{0:T(1024)S(1)}, s32[4096]{0:T(1024)}, u32[]{:S(2)}) copy-start(s32[4096]{0:T(1024)} %param.10) | copy-start | bytes 49156

commit v4 on v3

--- a/solution.py
+++ b/solution.py
@@ -166,7 +166,7 @@
     return copies
 
 
-def sum_small(axis, value, slots, sems):
+def sum_small(axis, value, slots, sems, between=None):
     n = lax.axis_size(axis)
     me = lax.axis_index(axis)
     slots[me] = value
@@ -182,12 +182,13 @@
         )
         copy.start()
         copies.append(copy)
+    after = None if between is None else between()
     for copy in copies:
         copy.wait()
     total = slots[0]
     for k in range(1, n):
         total = total + slots[k]
-    return total
+    return total if between is None else (total, after)
 
 
 def rows_kernel(axis, sums_ref, scale_ref, out_ref, half, landing, whole, scatter_sems, gather_sems):
@@ -225,8 +226,13 @@
     total, mine, sent = scatter_sums("src", sums_ref, half, landing, scatter_sems)
     own = (total / root_of(scale_ref[:, mine])).astype(jnp.bfloat16)
     whole[:, mine] = own
-    gathered = gather_start("src", whole, mine, gather_sems)
-    first = sum_small("src", gram(own.astype(jnp.float32)), slots_src, src_sems)
+    first, gathered = sum_small(
+        "src",
+        gram(own.astype(jnp.float32)),
+        slots_src,
+        src_sems,
+        lambda: gather_start("src", whole, mine, gather_sems),
+    )
     first = sum_small("dst", first, slots_dst, dst_sems)
     inverse = inverse_factor(first / box_total)
     for copy in sent:

time: 146 us -> 138 us (0.945)
  Pallas kernels: 142 us -> 134 us
    pallas_call x2, Pallas kernels: 65.8 us -> 58 us  [reduce_panel(): pl.pallas_call(functools.partial(panel_kernel, box_total), in_specs=[VMEM...]
where the time goes in v4:
time: 138 us
  Pallas kernels  134 us (97%)
  local copies, waits for them, and re-layouts  3.93 us (3%)
    pallas_call x2, Pallas kernels, reduce_panel(): pl.pallas_call(functools.partial(panel_kernel, box_total), in_specs=[VMEM...  58 us
    pallas_call x4, Pallas kernels, sweep(): pl.pallas_call(functools.partial(sweep_kernel, contract, unroll), in_spec...  47.5 us
    pallas_call x2, Pallas kernels, reduce_rows(): pl.pallas_call(functools.partial(rows_kernel, 'dst'), in_specs=[VMEM] * 2...  28.4 us
    unnamed x13, local copies, waits for them, and re-layouts  3.93 us

profile of v4, /device:TPU:0, one launch (start us, length us, event | category | flops | bytes accessed | tf_op | source)
XLA Modules:
  0.0 137.9 jit_solution(5529707432214602257)
XLA Ops:
  0.0 0.0 copy-start
  0.0 1.0 copy-done
  1.0 0.0 copy-start.1
  1.0 0.7 copy-done.1
  1.8 0.0 copy-start.4
  1.8 0.7 copy-done.4
  2.4 0.0 copy-start.5
  2.5 0.7 copy-done.5
  3.1 0.0 copy-start.3
  3.1 0.0 copy-start.2
  3.1 14.5 %shard_map.64.sums_ref = f32[32,8192]{1,0:T(8,128)S(1)} custom-call(s32[640]{0:T(1024)S(1)} %copy-done.5, s32[640]{0:T(1024)S(1)} %copy-done.4, f32[32,4096]{1,0:T(8,128)S(1)} %copy-done, s32[1,4096]{1,0:T(1,128)S(1)} %bitcast.2, bf16[640,128,128]{2,1,0:T(8,128)(2,1)} %refs_0_.3), custom_call_target="tpu_custom_call" | custom-call | tf_op jit(solution)/shard_map/pallas_call | solution.py:67
  17.7 0.0 copy-done.3
  17.7 15.3 %shard_map.65.panel_ref = bf16[32,8192]{1,0:T(8,128)(2,1)S(1)} custom-call(f32[32,8192]{1,0:T(8,128)S(1)} %shard_map.64.sums_ref, s32[1,8192]{1,0:T(1,128)S(1)} %bitcast.6), custom_call_target="tpu_custom_call" | custom-call | tf_op jit(solution)/shard_map/pallas_call | solution.py:254
  33.0 9.2 %shard_map.66.sums_ref = f32[32,4096]{1,0:T(8,128)S(1)} custom-call(s32[640]{0:T(1024)S(1)} %copy-done.4, s32[640]{0:T(1024)S(1)} %copy-done.5, bf16[32,8192]{1,0:T(8,128)(2,1)S(1)} %shard_map.65.panel_ref, bf16[640,128,128]{2,1,0:T(8,128)(2,1)} %refs_0_.3), custom_call_target="tpu_custom_call" | custom-call | tf_op jit(solution)/shard_map/pallas_call | solution.py:67
  42.2 0.0 copy-done.2
  42.2 29.3 %shard_map.67.panel_ref = f32[32,4096]{1,0:T(8,128)S(1)} custom-call(f32[32,4096]{1,0:T(8,128)S(1)} %shard_map.66.sums_ref, s32[1,4096]{1,0:T(1,128)S(1)} %bitcast.3), custom_call_target="tpu_custom_call" | custom-call | tf_op jit(solution)/shard_map/pallas_call | solution.py:276
  71.6 14.5 %shard_map.68.sums_ref = f32[32,8192]{1,0:T(8,128)S(1)} custom-call(s32[640]{0:T(1024)S(1)} %copy-done.5, s32[640]{0:T(1024)S(1)} %copy-done.4, f32[32,4096]{1,0:T(8,128)S(1)} %shard_map.67.panel_ref, s32[1,4096]{1,0:T(1,128)S(1)} %bitcast.4, bf16[640,128,128]{2,1,0:T(8,128)(2,1)} %refs_0_.3), custom_call_target="tpu_custom_call" | custom-call | tf_op jit(solution)/shard_map/pallas_call | solution.py:67
  86.1 13.1 %shard_map.69.panel_ref = bf16[32,8192]{1,0:T(8,128)(2,1)S(1)} custom-call(f32[32,8192]{1,0:T(8,128)S(1)} %shard_map.68.sums_ref, s32[1,8192]{1,0:T(1,128)S(1)} %bitcast.7), custom_call_target="tpu_custom_call" | custom-call | tf_op jit(solution)/shard_map/pallas_call | solution.py:254
  99.2 9.2 %shard_map.70.sums_ref = f32[32,4096]{1,0:T(8,128)S(1)} custom-call(s32[640]{0:T(1024)S(1)} %copy-done.4, s32[640]{0:T(1024)S(1)} %copy-done.5, bf16[32,8192]{1,0:T(8,128)(2,1)S(1)} %shard_map.69.panel_ref, bf16[640,128,128]{2,1,0:T(8,128)(2,1)} %refs_0_.3), custom_call_target="tpu_custom_call" | custom-call | tf_op jit(solution)/shard_map/pallas_call | solution.py:67
  108.4 28.7 %shard_map.71 = f32[32,4096]{1,0:T(8,128)S(1)} custom-call(f32[32,4096]{1,0:T(8,128)S(1)} %shard_map.70.sums_ref, s32[1,4096]{1,0:T(1,128)S(1)} %bitcast.5), custom_call_target="tpu_custom_call" | custom-call | tf_op jit(solution)/shard_map/pallas_call | solution.py:276
  137.1 0.8 copy.8
Async XLA Ops:
  0.0 1.0 copy-start
  1.0 0.7 copy-start.1
  1.8 0.7 copy-start.4
  2.4 0.7 copy-start.5
  3.1 14.5 %copy-start.3 = (s32[8192]{0:T(1024)S(1)}, s32[8192]{0:T(1024)}, u32[]{:S(2)}) copy-start(s32[8192]{0:T(1024)} %param.9) | copy-start | bytes 98308
  3.1 39.1 %copy-start.2 = (s32[4096]{0:T(1024)S(1)}, s32[4096]{0:T(1024)}, u32[]{:S(2)}) copy-start(s32[4096]{0:T(1024)} %param.10) | copy-start | bytes 49156
